TPU v7x, 128 devices: a whole 4x4x4 slice. The times are simulated.
128 devices in a mesh: flop: 8 (over z_hi, x), turn: 16 (over y, z_lo, core).
Axes of the slice: x: 4, y: 4, z: 4 (z_hi: 2, z_lo: 2; z = z_hi * 2 + z_lo), core: 2. Of those that a mesh axis runs over, the one named last changes fastest.
Arguments:
- trunk_regret: float32 [2, 7, 1408], P(None, None, 'turn'), may hold values from 0 to 0.02, as said below
- river_regret: float32 [32, 16, 8, 2, 2, 1408], P('flop', 'turn'), may hold values from 0.01 to 1
- line_pot: float32 [7], replicated, may hold values from 2 to 24
- subgame_line: int32 [32], P('flop'), may hold values from 0 to 6
- alive: int32 [32, 16, 8, 1408], P('flop', 'turn'), may hold values from 0 to 1, as said below
- ranks: int32 [32, 16, 8, 1408], P('flop', 'turn'), may hold values from 0 to 7461
Outputs:
- new_trunk: float32 [2, 7, 1408], P(None, None, 'turn')
- new_river: float32 [32, 16, 8, 2, 2, 1408], P('flop', 'turn')
Inputs may be any that keep to these rules, and one draw needn't show every extreme that they name: alive is 1 exactly for hand slots below 1326 whose two cards avoid the board: three flop cards common to a subgame, the turn card common to one turn index of it, and the river card; all these cards are distinct within a subgame. `trunk_regret`: for every player and hand slot some line has a positive regret.
All inputs are finite; a program needn't handle non-finite values.
Results may differ from a plain program's by a relative error of at most 0.0003.
Values sent between devices are 32-bit elements; how exact they have to be, the bound alone decides.
A program may use at most 64 MiB of HBM per device.

v0:
```python
import functools

import jax
import jax.numpy as jnp
import numpy as np
from jax import lax
from jax.experimental import pallas as pl
from jax.experimental.pallas import tpu as pltpu
from jax.sharding import PartitionSpec as P

CARDS = 52
BET_SIZE = 2.0
LANES = 128
BLOCK = 256
READY = 8
FRESH = 6
F32 = jnp.float32
BF16 = jnp.bfloat16
F8 = jnp.float8_e4m3fn
MESH = pl.DeviceIdType.MESH


def card_pairs(slot_count, card_count=CARDS):
    first_card, second_card = np.triu_indices(card_count, 1)
    extra = slot_count - first_card.shape[0]
    pad_first = -1 - 2 * np.arange(extra)
    pad_second = -2 - 2 * np.arange(extra)
    return (
        np.concatenate([first_card, pad_first]).astype(np.int32),
        np.concatenate([second_card, pad_second]).astype(np.int32),
    )


def compat_table(slot_count, card_count):
    first, second = card_pairs(slot_count, card_count)
    collide = (
        (first[:, None] == first[None, :])
        | (first[:, None] == second[None, :])
        | (second[:, None] == first[None, :])
        | (second[:, None] == second[None, :])
        | (first[:, None] < 0)
        | (first[None, :] < 0)
    )
    return np.where(collide, 0.0, 1.0).astype(np.float32)


def card_table(slot_count, card_count):
    first, second = card_pairs(slot_count, card_count)
    cards = np.arange(LANES)[None, :]
    return ((first[:, None] == cards) | (second[:, None] == cards)).astype(np.float32)


def shifted(index, step, size):
    high = lax.rem(lax.div(index, 4) + step // 4, size // 4)
    return high * 4 + lax.rem(lax.rem(index, 4) + step % 4, 4)


def far_first(size, distances):
    high, low = distances
    return sorted(range(1, size), key=lambda step: -(high[step // 4] + low[step % 4]))


def roll_lanes(x, shift):
    shift %= x.shape[-1]
    return pltpu.roll(x, shift, 1) if shift else x


def strategy_of(regret):
    return regret / jnp.sum(regret, axis=0, keepdims=True)


def blocks_of(size):
    return [(at, min(BLOCK, size - at)) for at in range(0, size, BLOCK)]


def tiles_of(array):
    return [array[:, at : at + LANES] for at in range(0, array.shape[1], LANES)]


def rank_code(ranks):
    octave = ranks >> 7
    small = (1 << (octave & 15)).astype(F32)
    large = jnp.where(
        octave >= 32,
        jnp.where(octave >= 48, 2.0**48, 2.0**32),
        jnp.where(octave >= 16, 2.0**16, 1.0),
    )
    return ((ranks & 127) + 128).astype(F32) * small * large


def table_blocks(size):
    sides = blocks_of(size)
    return [
        (start, depth, at, width)
        for number, (start, depth) in enumerate(sides)
        for at, width in sides[number:]
    ]


def product(rows, table, axis):
    return lax.dot_general(rows, table, (((1,), (axis,)), ((), ())), preferred_element_type=F32)


def three_parts(x):
    high = x.astype(BF16)
    rest = x - high.astype(F32)
    middle = rest.astype(BF16)
    low = (rest - middle.astype(F32)).astype(BF16)
    return jnp.concatenate([high, middle, low], axis=0)


def load_rows(ref, start, count, stride=1):
    rows = pl.ds(start, count, stride=stride)
    return jnp.concatenate([ref[tile, rows, :] for tile in range(ref.shape[0])], axis=1)


def store_rows(ref, start, count, stride, value):
    rows = pl.ds(start, count, stride=stride)
    for tile, part in enumerate(tiles_of(value)):
        ref[tile, rows, :] = part


def stack_rows(rows, count):
    return jnp.broadcast_to(rows[None], (count,) + rows.shape).reshape(
        count * rows.shape[0], rows.shape[1]
    )


def lanes_at(tiles, tile, source):
    lane = source & (LANES - 1)
    at = source >> 7
    found = None
    for number in tile:
        part = jnp.take_along_axis(tiles[number], lane, axis=1)
        found = part if found is None else jnp.where(at == number, part, found)
    return found


def prefix_counts(marks, ones_ref):
    tiles = tiles_of(marks)
    inner = jnp.dot(jnp.concatenate(tiles, axis=0).astype(BF16), ones_ref[...], preferred_element_type=F32)
    base = jnp.zeros((8, 1), F32)
    counts = []
    for number, tile in enumerate(tiles):
        counts.append(inner[number * 8 : number * 8 + 8] + base)
        base = base + jnp.sum(tile, axis=1, keepdims=True)
    return jnp.concatenate(counts, axis=1).astype(jnp.int32)


def iteration_kernel(
    flops, turns, scale,
    line_ref, pot_ref, trunk_ref, regret_hbm, alive_hbm, ranks_hbm, compat_hbm, cards_hbm, slots_hbm, ones_hbm,
    trunk_out, river_out,
    regret, alive, ranks, compat, cards, card_slots, ones, flat, sigma, fold, source, target, unblocked, open_slots,
    reach, table, left, sums, code, row_code, column_code, strategy, mine, shares, parts, pieces, values, lines_in,
    sems, out_sem, send_share, recv_share, send_part, recv_part, send_line, recv_line,
):
    flop, turn = lax.axis_index("flop"), lax.axis_index("turn")
    subgames, _, rivers, _, _, slots = regret.shape
    lines, _, share = trunk_ref.shape
    packed = compat.shape[0]
    hands = (CARDS - 4) * (CARDS - 5) // 2

    def turn_peer(step):
        return (flop, shifted(turn, step, turns))

    def flop_peer(step):
        return (shifted(flop, step, flops), turn)

    def remote(src, dst, send, recv, peer):
        return pltpu.make_async_remote_copy(
            src_ref=src, dst_ref=dst, send_sem=send, recv_sem=recv, device_id=peer, device_id_type=MESH
        )

    turn_steps = far_first(turns, ((0, 1, 2, 1), (0, 1, 1, 1)))
    flop_steps = far_first(flops, ((0, 2), (0, 1, 2, 1)))
    copies = [
        pltpu.make_async_copy(hbm, vmem, sems.at[number])
        for number, (hbm, vmem) in enumerate(
            [
                (alive_hbm, alive),
                (ones_hbm, ones),
                (ranks_hbm, ranks),
                (regret_hbm, regret),
                (cards_hbm, cards),
                (slots_hbm, card_slots),
                (compat_hbm, compat),
            ]
        )
    ]
    for copy in copies:
        copy.start()

    barrier = pltpu.get_barrier_semaphore()
    for step in turn_steps:
        pl.semaphore_signal(barrier, inc=1, device_id=turn_peer(step), device_id_type=MESH)
    for step in flop_steps:
        pl.semaphore_signal(barrier, inc=1, device_id=flop_peer(step), device_id_type=MESH)
    mine[...] = jnp.zeros_like(mine)
    own = [strategy_of(trunk_ref[:, player]) for player in range(2)]
    for player in range(2):
        mine[player * 8 : player * 8 + lines, :share] = own[player]
    pl.semaphore_wait(barrier, turns + flops - 2)
    sent = []
    for step in turn_steps:
        sent.append(
            remote(mine, shares.at[turn], send_share.at[step], recv_share.at[turn], turn_peer(step))
        )
        sent[-1].start()
    shares[turn] = mine[...]

    copies[0].wait()
    copies[1].wait()
    rows = [jnp.max(alive[s, 0].astype(F32), axis=0, keepdims=True) for s in range(subgames)]
    live_any = jnp.concatenate(rows + rows, axis=0)
    before = prefix_counts(1.0 - live_any, ones)
    slot = lax.broadcasted_iota(jnp.int32, (8, slots), 1)
    state = jnp.where(live_any > 0.5, before * 2048 + slot, 0)
    for bit in range(8):
        moved = pltpu.roll(state, slots - (1 << bit), 1)
        flag = 2048 << bit
        state = jnp.where((moved & flag) != 0, moved, jnp.where((state & flag) != 0, 0, state))
    store_rows(target, 0, 8, 1, slot - before)
    store_rows(unblocked, 0, 8, 1, live_any)
    store_rows(source, 0, 8, 1, (state & 2047)[:, :packed])

    def spread(ref, subgame):
        return [
            jnp.broadcast_to(ref[tile, pl.ds(subgame, 1), :], (8, LANES))
            for tile in range(ref.shape[0])
        ]

    def pack(tiles, sources):
        return jnp.concatenate(
            [lanes_at(tiles, (t, t + 1, t + 2), sources[t]) for t in range(packed // LANES)], axis=1
        )

    def unpack(tiles, targets):
        found = []
        for t in range(slots // LANES):
            near = [n for n in (t - 2, t - 1, t) if 0 <= n < packed // LANES]
            found.append(lanes_at(tiles, near, targets[t]))
        return jnp.concatenate(found, axis=1)

    for number in range(2, 6):
        copies[number].wait()

    def rounded(x):
        return x.astype(BF16).astype(F32)

    def prepare(subgame, carry):
        sources = spread(source, subgame)
        first = pl.multiple_of(subgame * rivers, rivers)
        base = pl.multiple_of(subgame * 4 * rivers, 4 * rivers)
        store_rows(code, first, rivers, 1, pack(tiles_of(rank_code(ranks[subgame, 0])), sources))
        for river in range(rivers):
            for player in range(2):
                store_rows(flat, base + river * 4 + player * 2, 2, 1, regret[subgame, 0, river, player])
        one_check, one_bet, two_fold, two_call = [
            pack(tiles_of(load_rows(flat, base + n, rivers, 4)), sources) for n in range(4)
        ]
        one_sum = one_check + one_bet
        two_sum = two_fold + two_call
        for number, part in enumerate(
            [one_check / one_sum, one_bet / one_sum, two_fold / two_sum, two_call / two_sum]
        ):
            store_rows(sigma, base + number, rivers, 4, part)
        at = lax.broadcasted_iota(jnp.int32, (rivers, packed), 1)
        live = pack(tiles_of(alive[subgame, 0].astype(F32)), sources)
        store_rows(open_slots, first, rivers, 1, jnp.where(at < hands, live, 0.0))
        return carry

    lax.fori_loop(0, subgames, prepare, 0)
    copies[6].wait()

    blocks = table_blocks(packed)

    def ready_codes(first, count):
        for which in range(count):
            codes = load_rows(code, first + which, 1)
            row_code[which] = jnp.broadcast_to(codes, (16, packed)).astype(BF16)
            tall = jnp.broadcast_to(codes, (LANES, packed)).astype(BF16)
            for at in range(0, packed, LANES):
                column_code[which, at : at + LANES, :] = jnp.transpose(tall[:, at : at + LANES])

    def sign_block(which, block, most):
        start, depth, at, width = block
        one = jnp.ones((), BF16)
        column = column_code[which, start : start + depth, :]
        column = jnp.concatenate([column] * (width // LANES), axis=1)
        row = stack_rows(row_code[which, :, at : at + width], depth // 16)
        return (jnp.maximum(jnp.minimum(row - column, one), -one) * most).astype(F8)

    def masks(block):
        start, depth, at, width = block
        return compat[start : start + depth, at : at + width]

    def play(boards, sign_of):
        lefts = [load_rows(left, pl.multiple_of(board * 8, 8), 8).astype(BF16) for board in boards]
        totals = {}

        def add(which, at, part):
            for number, piece in enumerate(tiles_of(part)):
                key = (which, at // LANES + number)
                totals[key] = totals[key] + piece if key in totals else piece

        for block in blocks:
            start, depth, at, width = block
            most = masks(block)
            for which in range(len(boards)):
                sign = sign_of(which, block, most)
                add(which, at, product(lefts[which][:, start : start + depth], sign, 0))
                if at > start:
                    add(which, start, -product(lefts[which][:, at : at + width], sign, 1))
        for which, board in enumerate(boards):
            rows = pl.ds(pl.multiple_of(board * 8, 8), 8)
            for number in range(packed // LANES):
                sums[number, rows, :] = totals[which, number]

    def tables(block):
        start, depth, at, width = block
        return [(slice(start, start + depth), at // LANES + n) for n in range(width // LANES)]

    def build_first():
        ready_codes(0, READY)
        for block in blocks:
            most = masks(block)
            for which in range(READY):
                for (rows, tile), part in zip(tables(block), tiles_of(sign_block(which, block, most))):
                    table[which, tile, rows, :] = part

    def built(which, block):
        return jnp.concatenate([table[which, tile, rows, :] for rows, tile in tables(block)], axis=1)

    steps = (subgames * rivers - READY) // FRESH
    ready = READY // steps

    def some_boards(step, carry):
        first = READY + step * FRESH
        ready_codes(first, FRESH)

        def sign_of(which, block, most):
            if which < FRESH:
                return sign_block(which, block, most)
            return built(step * ready + which - FRESH, block)

        play([first + n for n in range(FRESH)] + [step * ready + n for n in range(ready)], sign_of)
        return carry

    build_first()

    for step in turn_steps:
        peer = turn_peer(step)
        remote(mine, shares.at[peer[1]], send_share.at[step], recv_share.at[peer[1]], peer).wait_recv()
    lane = lax.broadcasted_iota(jnp.int32, (16, LANES), 1)
    tiles = [None] * (slots // LANES)
    for number in range(turns):
        tile, offset = divmod(number * share, LANES)
        piece = roll_lanes(shares[number], offset)
        low = jnp.where(lane >= offset, piece, 0.0) if offset else piece
        tiles[tile] = low if tiles[tile] is None else tiles[tile] + low
        if offset + share > LANES:
            tiles[tile + 1] = jnp.where(lane < offset + share - LANES, piece, 0.0)
    for tile, value in enumerate(tiles):
        strategy[:, tile * LANES : (tile + 1) * LANES] = value
    chosen = [
        strategy[pl.ds(8 * player + line_ref[subgame], 1), :]
        for player in range(2)
        for subgame in range(subgames)
    ]
    chosen = tiles_of(jnp.concatenate(chosen, axis=0))
    store_rows(reach, 0, 8, 1, pack(chosen, [source[t] for t in range(packed // LANES)]))

    def enter(subgame, carry):
        first = pl.multiple_of(subgame * rivers, rivers)
        base = pl.multiple_of(subgame * 4 * rivers, 4 * rivers)
        reach_one = load_rows(reach, subgame, 1)
        reach_two = load_rows(reach, subgames + subgame, 1)
        live = load_rows(open_slots, first, rivers)
        sigma_check, sigma_bet, sigma_fold, sigma_call = [
            load_rows(sigma, base + n, rivers, 4) for n in range(4)
        ]
        in_bet = rounded(live * (reach_one * sigma_bet))
        in_fold = rounded(live * (reach_two * sigma_fold))
        shows = [
            live * reach_two,
            live * (reach_two * sigma_call),
            in_bet,
            live * (reach_one * sigma_check),
        ]
        start = pl.multiple_of(subgame * 8 * rivers, 8 * rivers)
        for number, value in enumerate(shows):
            store_rows(left, start + number, rivers, 8, value)
            store_rows(left, start + 4 + number, rivers, 8, jnp.zeros((rivers, packed), F32))
        fold_in = jnp.concatenate([in_fold, in_bet], axis=0)
        per_card = jnp.dot(fold_in.astype(BF16), cards[...], preferred_element_type=F32)
        per_slot = jnp.dot(three_parts(per_card), card_slots[...], preferred_element_type=F32)
        count = fold_in.shape[0]
        per_slot = per_slot[:count] + per_slot[count : 2 * count] + per_slot[2 * count :]
        fold_sums = jnp.sum(fold_in, axis=1, keepdims=True) - per_slot + fold_in
        store_rows(fold, pl.multiple_of(subgame * 2 * rivers, 2 * rivers), 2 * rivers, 1, fold_sums)
        return carry

    lax.fori_loop(0, subgames, enter, 0)

    lax.fori_loop(0, steps, some_boards, 0)

    def leave(subgame, carry):
        first = pl.multiple_of(subgame * rivers, rivers)
        base = pl.multiple_of(subgame * 4 * rivers, 4 * rivers)
        start = pl.multiple_of(subgame * 8 * rivers, 8 * rivers)
        half_pot = 0.5 * pot_ref[line_ref[subgame]]
        call_pot = half_pot + BET_SIZE
        live = load_rows(open_slots, first, rivers)
        weight = live * (1.0 / ((CARDS - 7) * (CARDS - 8) / 2.0))
        show = [load_rows(sums, start + number, rivers, 8) * weight for number in range(4)]
        fold_sums = load_rows(fold, pl.multiple_of(subgame * 2 * rivers, 2 * rivers), 2 * rivers)
        fold_two, fold_one = fold_sums[:rivers] * weight, fold_sums[rivers:] * weight
        sigma_check, sigma_bet, sigma_fold, sigma_call = [
            load_rows(sigma, base + n, rivers, 4) for n in range(4)
        ]
        check_value = half_pot * show[0]
        bet_value = half_pot * fold_two + call_pot * show[1]
        fold_value = -half_pot * fold_one
        call_value = call_pot * show[2]
        check_line = half_pot * show[3]
        one_node = sigma_check * check_value + sigma_bet * bet_value
        two_node = sigma_fold * fold_value + sigma_call * call_value
        for number, value in enumerate(
            [check_value - one_node, bet_value - one_node, fold_value - two_node, call_value - two_node]
        ):
            store_rows(sigma, base + number, rivers, 4, value)
        roots = [
            jnp.sum(one_node, axis=0, keepdims=True),
            jnp.sum(check_line + two_node, axis=0, keepdims=True),
        ]
        for player in range(2):
            store_rows(values, player * subgames + subgame, 1, 1, roots[player])
        return carry

    lax.fori_loop(0, subgames, leave, 0)

    lane = lax.broadcasted_iota(jnp.int32, (8, LANES), 1)
    roots = [values[t] for t in range(packed // LANES)]
    roots = tiles_of(unpack(roots, [target[t] for t in range(slots // LANES)]))
    roots = [part * unblocked[t] for t, part in enumerate(roots)]
    for number in range(turns):
        tile, offset = divmod(number * share, LANES)
        piece = roll_lanes(roots[tile], -offset)
        if offset + share > LANES:
            after = roll_lanes(roots[tile + 1], -offset)
            piece = jnp.where(lane < LANES - offset, piece, after)
        parts[number] = piece
    for step in turn_steps:
        peer = turn_peer(step)
        sent.append(
            remote(parts.at[peer[1]], pieces.at[turn], send_part.at[step], recv_part.at[turn], peer)
        )
        sent[-1].start()
    pieces[turn] = parts[turn]

    def write(subgame, carry):
        targets = spread(target, subgame)
        base = pl.multiple_of(subgame * 4 * rivers, 4 * rivers)
        live = alive[subgame, 0].astype(F32)
        for number in range(4):
            change = unpack(tiles_of(load_rows(sigma, base + number, rivers, 4)), targets) * live
            value = jnp.maximum(load_rows(flat, base + number, rivers, 4) + change, 0.0)
            store_rows(flat, base + number, rivers, 4, value)
        for river in range(rivers):
            for player in range(2):
                regret[subgame, 0, river, player] = load_rows(flat, base + river * 4 + player * 2, 2)
        return carry

    lax.fori_loop(0, subgames, write, 0)
    out_copy = pltpu.make_async_copy(regret, river_out, out_sem)
    out_copy.start()

    for step in turn_steps:
        peer = turn_peer(step)
        remote(
            parts.at[peer[1]], pieces.at[peer[1]], send_part.at[step], recv_part.at[peer[1]], peer
        ).wait_recv()
    root = pieces[0]
    for number in range(1, turns):
        root = root + pieces[number]
    row = lax.broadcasted_iota(jnp.int32, (8, LANES), 0)
    for player in range(2):
        by_line = jnp.zeros((8, LANES), F32)
        for subgame in range(subgames):
            at = player * subgames + subgame
            by_line = by_line + jnp.where(row == line_ref[subgame], root[at : at + 1, :], 0.0)
        mine_lines = lines_in.at[flop]
        mine_lines[player * 8 : player * 8 + 8, :] = by_line
    for step in flop_steps:
        sent.append(
            remote(
                lines_in.at[flop], lines_in.at[flop], send_line.at[step], recv_line.at[flop], flop_peer(step)
            )
        )
        sent[-1].start()
    for step in flop_steps:
        peer = flop_peer(step)
        remote(
            lines_in.at[flop], lines_in.at[peer[0]], send_line.at[step], recv_line.at[peer[0]], peer
        ).wait_recv()
    total = lines_in[0]
    for number in range(1, flops):
        total = total + lines_in[number]
    total = total * scale
    for player in range(2):
        line_values = total[player * 8 : player * 8 + lines, :share]
        node = jnp.sum(own[player] * line_values, axis=0, keepdims=True)
        trunk_out[:, player] = jnp.maximum(trunk_ref[:, player] + line_values - node, 0.0)
    out_copy.wait()
    for copy in sent:
        copy.wait_send()


def on_device(flops, turns, trunk_regret, river_regret, line_pot, subgame_line, alive, ranks):
    subgames, turn_local, rivers, _, _, slots = river_regret.shape
    lines = trunk_regret.shape[1]
    scale = lines / (subgames * flops * turn_local * turns * rivers)
    packed = -(-((CARDS - 4) * (CARDS - 5) // 2) // LANES) * LANES
    compat = jnp.asarray(compat_table(packed, CARDS - 4).astype(jnp.bfloat16))
    cards = jnp.asarray(card_table(packed, CARDS - 4).astype(jnp.bfloat16))
    card_slots = jnp.asarray(card_table(packed, CARDS - 4).T.astype(jnp.bfloat16))
    ones = jnp.asarray(np.triu(np.ones((LANES, LANES)), 1).astype(jnp.bfloat16))
    by_line = trunk_regret.transpose(1, 0, 2)
    smem = pl.BlockSpec(memory_space=pltpu.SMEM)
    vmem = pl.BlockSpec(memory_space=pltpu.VMEM)
    hbm = pl.BlockSpec(memory_space=pl.ANY)
    boards = subgames * rivers
    tiles, packed_tiles = slots // LANES, packed // LANES
    rows = lambda count, tile_count=tiles: pltpu.VMEM((tile_count, count, LANES), F32)
    dma = lambda *shape: pltpu.SemaphoreType.DMA(shape)
    new_trunk, new_river = pl.pallas_call(
        functools.partial(iteration_kernel, flops, turns, scale),
        out_shape=(
            jax.ShapeDtypeStruct(by_line.shape, F32),
            jax.ShapeDtypeStruct(river_regret.shape, F32),
        ),
        in_specs=[smem, smem, vmem] + [hbm] * 7,
        out_specs=(vmem, hbm),
        scratch_shapes=[
            pltpu.VMEM(river_regret.shape, F32),
            pltpu.VMEM(alive.shape, jnp.int32),
            pltpu.VMEM(ranks.shape, jnp.int32),
            pltpu.VMEM(compat.shape, BF16),
            pltpu.VMEM(cards.shape, BF16),
            pltpu.VMEM(card_slots.shape, BF16),
            pltpu.VMEM(ones.shape, BF16),
            rows(4 * boards),
            rows(4 * boards, packed_tiles),
            rows(2 * boards, packed_tiles),
            pltpu.VMEM((packed_tiles, 8, LANES), jnp.int32),
            pltpu.VMEM((tiles, 8, LANES), jnp.int32),
            rows(8),
            rows(boards, packed_tiles),
            rows(8, packed_tiles),
            pltpu.VMEM((READY, packed_tiles, packed, LANES), F8),
            rows(8 * boards, packed_tiles),
            rows(8 * boards, packed_tiles),
            rows(boards, packed_tiles),
            pltpu.VMEM((READY, 16, packed), BF16),
            pltpu.VMEM((READY, packed, LANES), BF16),
            pltpu.VMEM((16, slots), F32),
            pltpu.VMEM((16, LANES), F32),
            rows(16, turns),
            rows(8, turns),
            rows(8, turns),
            rows(8, packed_tiles),
            rows(16, flops),
            dma(7),
            pltpu.SemaphoreType.DMA,
            dma(turns),
            dma(turns),
            dma(turns),
            dma(turns),
            dma(flops),
            dma(flops),
        ],
        compiler_params=pltpu.CompilerParams(
            collective_id=0, has_side_effects=True, vmem_limit_bytes=60 * 2**20
        ),
        name="cfr_iteration",
    )(subgame_line, line_pot, by_line, river_regret, alive, ranks, compat, cards, card_slots, ones)
    return (new_trunk.transpose(1, 0, 2), new_river)


def solution(mesh):
    return jax.shard_map(
        functools.partial(on_device, mesh.shape["flop"], mesh.shape["turn"]),
        mesh=mesh,
        in_specs=(
            P(None, None, "turn"),
            P("flop", "turn", None, None, None, None),
            P(),
            P("flop"),
            P("flop", "turn", None, None),
            P("flop", "turn", None, None),
        ),
        out_specs=(P(None, None, "turn"), P("flop", "turn", None, None, None, None)),
        check_vma=False,
    )
```

profile of v0, /device:TPU:1, one launch (start us, length us, event | category | flops | bytes accessed | tf_op | source)
XLA Modules:
  0.0 40.1 jit_solution(2973493314302080799)
XLA Ops:
  0.6 36.1 %cfr_iteration.1 = (f32[7,2,88]{2,1,0:T(2,128)}, f32[4,1,8,2,2,1408]{5,4,3,2,1,0:T(2,128)}) custom-call(s32[4]{0:T(128)} %line_ref.1, f32[7]{0:T(128)} %pot_ref.1, f32[7,2,88]{2,1,0:T(2,128)} %bitcast.2, f32[4,1,8,2,2,1408]{5,4,3,2,1,0:T(2,128)} %regret_hbm.1, s32[4,1,8,1408]{3,2,1,0:T(8,128)} %alive_hbm.1, s32[4,1,8,1408]{3,2,1,0:T(8,128)} %ranks_hbm.1, ...), custom_call_target="tpu_custom_call" | custom-call | tf_op jit(solution)/shard_map/cfr_iteration/pallas_call | solution.py:537
  36.8 1.3 %copy.14 = f32[2,7,88]{2,0,1:T(2,128)} copy(f32[2,7,88]{2,0,1:T(2,128)} %bitcast.3) | data formatting | bytes 9856
  38.0 2.1 %copy.15 = f32[4,1,8,2,2,1408]{5,4,3,2,1,0:T(2,128)} copy(f32[4,1,8,2,2,1408]{5,4,3,2,1,0:T(2,128)} %get-tuple-element.9) | data formatting | bytes 1441792
where the time goes:
time: 40.3 us; the launch traced here: 40.1 us
  Pallas kernels  36.1 us (90%)
  local copies, waits for them, and re-layouts  3.34 us (8%)
  between operations  0.64 us (2%)
    pallas_call x1, Pallas kernels, on_device(): pl.pallas_call(functools.partial(iteration_kernel, flops, turns, scale),...  36.1 us
    unnamed x2, local copies, waits for them, and re-layouts  3.34 us

commit v1 on v0

--- a/solution.py
+++ b/solution.py
@@ -149,9 +149,9 @@
 
 def iteration_kernel(
     flops, turns, scale,
-    line_ref, pot_ref, trunk_ref, regret_hbm, alive_hbm, ranks_hbm, compat_hbm, cards_hbm, slots_hbm, ones_hbm,
+    line_hbm, pot_hbm, trunk_hbm, regret_hbm, alive_hbm, ranks_hbm, compat_hbm, cards_hbm, slots_hbm, ones_hbm,
     trunk_out, river_out,
-    regret, alive, ranks, compat, cards, card_slots, ones, flat, sigma, fold, source, target, unblocked, open_slots,
+    line_ref, pot_ref, trunk_ref, regret, alive, ranks, compat, cards, card_slots, ones, flat, sigma, fold, source, target, unblocked, open_slots,
     reach, table, left, sums, code, row_code, column_code, strategy, mine, shares, parts, pieces, values, lines_in,
     sems, out_sem, send_share, recv_share, send_part, recv_part, send_line, recv_line,
 ):
@@ -174,10 +174,18 @@
 
     turn_steps = far_first(turns, ((0, 1, 2, 1), (0, 1, 1, 1)))
     flop_steps = far_first(flops, ((0, 2), (0, 1, 2, 1)))
+    barrier = pltpu.get_barrier_semaphore()
+    for step in turn_steps:
+        pl.semaphore_signal(barrier, inc=1, device_id=turn_peer(step), device_id_type=MESH)
+    for step in flop_steps:
+        pl.semaphore_signal(barrier, inc=1, device_id=flop_peer(step), device_id_type=MESH)
     copies = [
         pltpu.make_async_copy(hbm, vmem, sems.at[number])
         for number, (hbm, vmem) in enumerate(
             [
+                (trunk_hbm, trunk_ref),
+                (line_hbm, line_ref),
+                (pot_hbm, pot_ref),
                 (alive_hbm, alive),
                 (ones_hbm, ones),
                 (ranks_hbm, ranks),
@@ -191,12 +199,8 @@
     for copy in copies:
         copy.start()
 
-    barrier = pltpu.get_barrier_semaphore()
-    for step in turn_steps:
-        pl.semaphore_signal(barrier, inc=1, device_id=turn_peer(step), device_id_type=MESH)
-    for step in flop_steps:
-        pl.semaphore_signal(barrier, inc=1, device_id=flop_peer(step), device_id_type=MESH)
     mine[...] = jnp.zeros_like(mine)
+    copies[0].wait()
     own = [strategy_of(trunk_ref[:, player]) for player in range(2)]
     for player in range(2):
         mine[player * 8 : player * 8 + lines, :share] = own[player]
@@ -209,8 +213,8 @@
         sent[-1].start()
     shares[turn] = mine[...]
 
-    copies[0].wait()
-    copies[1].wait()
+    copies[3].wait()
+    copies[4].wait()
     rows = [jnp.max(alive[s, 0].astype(F32), axis=0, keepdims=True) for s in range(subgames)]
     live_any = jnp.concatenate(rows + rows, axis=0)
     before = prefix_counts(1.0 - live_any, ones)
@@ -242,7 +246,7 @@
             found.append(lanes_at(tiles, near, targets[t]))
         return jnp.concatenate(found, axis=1)
 
-    for number in range(2, 6):
+    for number in (1, 2, 5, 6, 7, 8):
         copies[number].wait()
 
     def rounded(x):
@@ -271,7 +275,7 @@
         return carry
 
     lax.fori_loop(0, subgames, prepare, 0)
-    copies[6].wait()
+    copies[9].wait()
 
     blocks = table_blocks(packed)
 
@@ -335,7 +339,19 @@
     steps = (subgames * rivers - READY) // FRESH
     ready = READY // steps
 
+    def add_folds(subgame):
+        start = pl.multiple_of(subgame * 8 * rivers, 8 * rivers)
+        fold_in = jnp.concatenate([load_rows(left, start + n, rivers, 8) for n in (4, 2)], axis=0)
+        per_card = jnp.dot(fold_in.astype(BF16), cards[...], preferred_element_type=F32)
+        per_slot = jnp.dot(three_parts(per_card), card_slots[...], preferred_element_type=F32)
+        count = fold_in.shape[0]
+        per_slot = per_slot[:count] + per_slot[count : 2 * count] + per_slot[2 * count :]
+        fold_sums = jnp.sum(fold_in, axis=1, keepdims=True) - per_slot + fold_in
+        store_rows(fold, pl.multiple_of(subgame * 2 * rivers, 2 * rivers), 2 * rivers, 1, fold_sums)
+
     def some_boards(step, carry):
+        for number in range(subgames // steps):
+            add_folds(step * (subgames // steps) + number)
         first = READY + step * FRESH
         ready_codes(first, FRESH)
 
@@ -389,16 +405,9 @@
             live * (reach_one * sigma_check),
         ]
         start = pl.multiple_of(subgame * 8 * rivers, 8 * rivers)
-        for number, value in enumerate(shows):
+        none = jnp.zeros((rivers, packed), F32)
+        for number, value in enumerate(shows + [in_fold, none, none, none]):
             store_rows(left, start + number, rivers, 8, value)
-            store_rows(left, start + 4 + number, rivers, 8, jnp.zeros((rivers, packed), F32))
-        fold_in = jnp.concatenate([in_fold, in_bet], axis=0)
-        per_card = jnp.dot(fold_in.astype(BF16), cards[...], preferred_element_type=F32)
-        per_slot = jnp.dot(three_parts(per_card), card_slots[...], preferred_element_type=F32)
-        count = fold_in.shape[0]
-        per_slot = per_slot[:count] + per_slot[count : 2 * count] + per_slot[2 * count :]
-        fold_sums = jnp.sum(fold_in, axis=1, keepdims=True) - per_slot + fold_in
-        store_rows(fold, pl.multiple_of(subgame * 2 * rivers, 2 * rivers), 2 * rivers, 1, fold_sums)
         return carry
 
     lax.fori_loop(0, subgames, enter, 0)
@@ -527,7 +536,6 @@
     card_slots = jnp.asarray(card_table(packed, CARDS - 4).T.astype(jnp.bfloat16))
     ones = jnp.asarray(np.triu(np.ones((LANES, LANES)), 1).astype(jnp.bfloat16))
     by_line = trunk_regret.transpose(1, 0, 2)
-    smem = pl.BlockSpec(memory_space=pltpu.SMEM)
     vmem = pl.BlockSpec(memory_space=pltpu.VMEM)
     hbm = pl.BlockSpec(memory_space=pl.ANY)
     boards = subgames * rivers
@@ -540,9 +548,12 @@
             jax.ShapeDtypeStruct(by_line.shape, F32),
             jax.ShapeDtypeStruct(river_regret.shape, F32),
         ),
-        in_specs=[smem, smem, vmem] + [hbm] * 7,
+        in_specs=[hbm] * 10,
         out_specs=(vmem, hbm),
         scratch_shapes=[
+            pltpu.SMEM(subgame_line.shape, jnp.int32),
+            pltpu.SMEM(line_pot.shape, F32),
+            pltpu.VMEM(by_line.shape, F32),
             pltpu.VMEM(river_regret.shape, F32),
             pltpu.VMEM(alive.shape, jnp.int32),
             pltpu.VMEM(ranks.shape, jnp.int32),
@@ -571,7 +582,7 @@
             rows(8, turns),
             rows(8, packed_tiles),
             rows(16, flops),
-            dma(7),
+            dma(10),
             pltpu.SemaphoreType.DMA,
             dma(turns),
             dma(turns),

time: 40.3 us -> 39 us (0.968)
  Pallas kernels: 36.1 us -> 34.9 us
    pallas_call x1, Pallas kernels: 36.1 us -> 34.9 us  [on_device(): pl.pallas_call(functools.partial(iteration_kernel, flops, turns, scale),...]
where the time goes in v1:
time: 39 us; the launch traced here: 38.8 us
  Pallas kernels  34.9 us (89%)
  local copies, waits for them, and re-layouts  3.34 us (9%)
  between operations  0.64 us (2%)
    pallas_call x1, Pallas kernels, on_device(): pl.pallas_call(functools.partial(iteration_kernel, flops, turns, scale),...  34.9 us
    unnamed x2, local copies, waits for them, and re-layouts  3.34 us

profile of v1, /device:TPU:1, one launch (start us, length us, event | category | flops | bytes accessed | tf_op | source)
XLA Modules:
  0.0 38.8 jit_solution(9746409263489852728)
XLA Ops:
  0.6 34.9 %cfr_iteration.1 = (f32[7,2,88]{2,1,0:T(2,128)}, f32[4,1,8,2,2,1408]{5,4,3,2,1,0:T(2,128)}) custom-call(s32[4]{0:T(128)} %line_hbm.1, f32[7]{0:T(128)} %pot_hbm.1, f32[7,2,88]{2,1,0:T(2,128)} %bitcast.2, f32[4,1,8,2,2,1408]{5,4,3,2,1,0:T(2,128)} %regret_hbm.1, s32[4,1,8,1408]{3,2,1,0:T(8,128)} %alive_hbm.1, s32[4,1,8,1408]{3,2,1,0:T(8,128)} %ranks_hbm.1, ...), custom_call_target="tpu_custom_call" | custom-call | tf_op jit(solution)/shard_map/cfr_iteration/pallas_call | solution.py:545
  35.5 1.3 %copy.14 = f32[2,7,88]{2,0,1:T(2,128)} copy(f32[2,7,88]{2,0,1:T(2,128)} %bitcast.3) | data formatting | bytes 9856
  36.8 2.1 %copy.15 = f32[4,1,8,2,2,1408]{5,4,3,2,1,0:T(2,128)} copy(f32[4,1,8,2,2,1408]{5,4,3,2,1,0:T(2,128)} %get-tuple-element.9) | data formatting | bytes 1441792

commit v2 on v1

--- a/solution.py
+++ b/solution.py
@@ -410,7 +410,7 @@
             store_rows(left, start + number, rivers, 8, value)
         return carry
 
-    lax.fori_loop(0, subgames, enter, 0)
+    lax.fori_loop(0, subgames, enter, 0, unroll=True)
 
     lax.fori_loop(0, steps, some_boards, 0)
 
@@ -447,7 +447,7 @@
             store_rows(values, player * subgames + subgame, 1, 1, roots[player])
         return carry
 
-    lax.fori_loop(0, subgames, leave, 0)
+    lax.fori_loop(0, subgames, leave, 0, unroll=True)
 
     lane = lax.broadcasted_iota(jnp.int32, (8, LANES), 1)
     roots = [values[t] for t in range(packed // LANES)]

time: 39 us -> 38.9 us (level)
  no operation moved by 1% of the time
where the time goes in v2:
time: 38.9 us; the launch traced here: 38.7 us
  Pallas kernels  34.7 us (89%)
  local copies, waits for them, and re-layouts  3.34 us (9%)
  between operations  0.64 us (2%)
    pallas_call x1, Pallas kernels, on_device(): pl.pallas_call(functools.partial(iteration_kernel, flops, turns, scale),...  34.7 us
    unnamed x2, local copies, waits for them, and re-layouts  3.34 us

profile of v2, /device:TPU:1, one launch (start us, length us, event | category | flops | bytes accessed | tf_op | source)
XLA Modules:
  0.0 38.7 jit_solution(6836761447951042746)
XLA Ops:
  0.6 34.7 %cfr_iteration.1 = (f32[7,2,88]{2,1,0:T(2,128)}, f32[4,1,8,2,2,1408]{5,4,3,2,1,0:T(2,128)}) custom-call(s32[4]{0:T(128)} %line_hbm.1, f32[7]{0:T(128)} %pot_hbm.1, f32[7,2,88]{2,1,0:T(2,128)} %bitcast.2, f32[4,1,8,2,2,1408]{5,4,3,2,1,0:T(2,128)} %regret_hbm.1, s32[4,1,8,1408]{3,2,1,0:T(8,128)} %alive_hbm.1, s32[4,1,8,1408]{3,2,1,0:T(8,128)} %ranks_hbm.1, ...), custom_call_target="tpu_custom_call" | custom-call | tf_op jit(solution)/shard_map/cfr_iteration/pallas_call | solution.py:545
  35.3 1.3 %copy.14 = f32[2,7,88]{2,0,1:T(2,128)} copy(f32[2,7,88]{2,0,1:T(2,128)} %bitcast.3) | data formatting | bytes 9856
  36.6 2.1 %copy.15 = f32[4,1,8,2,2,1408]{5,4,3,2,1,0:T(2,128)} copy(f32[4,1,8,2,2,1408]{5,4,3,2,1,0:T(2,128)} %get-tuple-element.9) | data formatting | bytes 1441792
